TPU v7x, 32 devices: a whole 2x2x4 slice. The times are simulated.
32 devices in a mesh: groups: 2 (over y), tp: 4 (over z), seq: 2 (over x), rep: 2 (over core).
Axes of the slice: x: 2, y: 2, z: 4, core: 2. Of those that a mesh axis runs over, the one named last changes fastest.
Arguments:
- queries: bfloat16 [2048, 8192], P(('groups', 'seq', 'rep'), 'tp'), parts along dimension 0, may hold values from -6 to 6
- keys: bfloat16 [2048, 8, 128], P(('groups', 'seq', 'rep')), parts along dimension 0, may hold values from -6 to 6
- values: bfloat16 [2048, 8, 128], P(('groups', 'seq', 'rep')), parts along dimension 0, may hold values from -18 to 18
- span_order: int32 [8], replicated, may hold values from 0 to 7, each once
- out_weight: bfloat16 [8192, 8192], P('tp', ('seq', 'rep')), may hold values from -0.0625 to 0.0625
- residual: bfloat16 [2048, 8192], P(('groups', 'seq', 'rep'), 'tp'), parts along dimension 0, may hold values from -30 to 30
- norm_gain: bfloat16 [8192], replicated, may hold values from 0.099609375 to 1.8984375
Outputs:
- stream: bfloat16 [2048, 8192], P(('groups', 'seq', 'rep'), 'tp'), parts along dimension 0
- normed: bfloat16 [2048, 8192], P(('groups', 'seq', 'rep')), parts along dimension 0
There are 2 independent parts, one for each index of `groups`. A program takes and returns all parts, laid end to end along the dimension named above; an argument that names none is the same for every part. Nothing has to cross between parts.
Inputs may be any that keep to these rules, and one draw needn't show every extreme that they name: A permutation: row block c of every token array, of 128 rows, holds prompt positions span_order[c] * 128 to span_order[c] * 128 + 127.
All inputs are finite; a program needn't handle non-finite values.
Results may differ from a plain program's by a relative error of at most 0.008.
Values may be sent and summed in bfloat16 or wider, within the bound.
A program may use at most 128 MiB of HBM per device.

v0:
```python
import math

import jax
import jax.numpy as jnp
from jax import lax
from jax.sharding import PartitionSpec as P

D = 8192
HQ = 64
KVH = 8


NEG_LARGE = -1e30
EPS_NORM = 1e-05


def positions(rows, span_order, span_len):
    blocks = rows // span_len
    numbers = lax.iota(jnp.int32, span_order.shape[0])
    chosen = jnp.sum(jnp.where(blocks[:, None] == numbers[None, :], span_order[None, :], 0), axis=1)
    return chosen * span_len + rows % span_len


def normalize(stream_rows, gain_part, square_total):
    stream_wide = stream_rows.astype(jnp.float32)
    inverse = lax.rsqrt(square_total[:, None] / D + EPS_NORM)
    return (stream_wide * inverse * gain_part.astype(jnp.float32)[None, :]).astype(jnp.bfloat16)


def on_device(queries, keys, values, span_order, out_weight, residual, norm_gain):
    tok_rows = queries.shape[0]
    head_size = keys.shape[2]
    heads_here = queries.shape[1] // head_size
    group_size = HQ // KVH
    per_group = min(group_size, heads_here)
    groups_here = heads_here // per_group
    span_len = tok_rows // 2
    tp_index = lax.axis_index("tp")
    kv_first = tp_index * heads_here // group_size
    key_sel = lax.dynamic_slice_in_dim(keys, kv_first, groups_here, 1).reshape(
        tok_rows, groups_here * head_size
    )
    value_sel = lax.dynamic_slice_in_dim(values, kv_first, groups_here, 1).reshape(
        tok_rows, groups_here * head_size
    )
    seq_index = lax.axis_index(("seq", "rep"))
    query_pos = positions(
        seq_index * tok_rows + lax.iota(jnp.int32, tok_rows), span_order, span_len
    )
    grouped = queries.reshape(tok_rows, groups_here, per_group, head_size)
    score_scale = 1.0 / math.sqrt(head_size)
    key_block = lax.all_gather(key_sel, ("seq", "rep"), axis=0, tiled=True)
    value_block = lax.all_gather(value_sel, ("seq", "rep"), axis=0, tiled=True)
    count = key_block.shape[0]
    key_pos = positions(lax.iota(jnp.int32, count), span_order, span_len)
    best = jnp.full((groups_here, per_group, tok_rows), NEG_LARGE, jnp.float32)
    keys_three = key_block.reshape(count, groups_here, head_size)
    values_three = value_block.reshape(count, groups_here, head_size)
    scores = (
        jnp.einsum("qgrd,kgd->grqk", grouped, keys_three, preferred_element_type=jnp.float32)
        * score_scale
    )
    allowed = key_pos[None, None, None, :] <= query_pos[None, None, :, None]
    scores = jnp.where(allowed, scores, NEG_LARGE)
    new_best = jnp.maximum(best, jnp.max(scores, axis=3))
    expo = jnp.where(allowed, jnp.exp(scores - new_best[..., None]), 0.0)
    new_totals = jnp.sum(expo, axis=3)
    update = jnp.einsum(
        "grqk,kgd->grqd",
        expo.astype(jnp.bfloat16),
        values_three,
        preferred_element_type=jnp.float32,
    )
    attention = (
        (update / new_totals[..., None])
        .transpose(2, 0, 1, 3)
        .reshape(tok_rows, heads_here * head_size)
        .astype(jnp.bfloat16)
    )
    term = jnp.dot(
        attention,
        lax.all_gather(out_weight, ("seq", "rep"), axis=1, tiled=True),
        preferred_element_type=jnp.float32,
    )
    width = residual.shape[1]
    summed = lax.psum_scatter(
        term.astype(jnp.bfloat16), "tp", scatter_dimension=1, tiled=True
    ).astype(jnp.float32)
    stream = (residual.astype(jnp.float32) + summed).astype(jnp.bfloat16)
    stream_wide = stream.astype(jnp.float32)
    square_total = lax.psum(jnp.sum(stream_wide * stream_wide, axis=1), "tp")
    gain_part = lax.dynamic_slice_in_dim(norm_gain, tp_index * width, width)
    normed_part = normalize(stream, gain_part, square_total)
    normed = lax.all_gather(normed_part, "tp", axis=1, tiled=True)
    return (stream, normed)


def solution(mesh):
    placed = (
        P(("groups", "seq", "rep"), "tp"),
        P(("groups", "seq", "rep"), None, None),
        P(("groups", "seq", "rep"), None, None),
        P(),
        P("tp", ("seq", "rep")),
        P(("groups", "seq", "rep"), "tp"),
        P(),
    )
    return jax.shard_map(
        on_device,
        mesh=mesh,
        in_specs=placed,
        out_specs=(P(("groups", "seq", "rep"), "tp"), P(("groups", "seq", "rep"), None)),
        check_vma=False,
    )
```

profile of v0, /device:TPU:0, one launch (start us, length us, event | category | flops | bytes accessed | tf_op | source)
XLA Modules:
  0.0 411.8 jit_solution(370616609168863187)
XLA Ops:
  7.2 0.0 all-gather.3.cloned.1.call-start
  7.2 0.7 all-gather.3.cloned.1.call-update
  7.9 0.0 reduce-scatter.2.cloned.1.call-start
  8.0 1.5 constant_dynamic-slice_fusion
  9.4 0.1 copy.27
  9.6 1.5 copy.28
  11.0 0.1 copy.26
  11.2 0.7 select_reduce_fusion.1
  11.9 0.7 select_reduce_fusion
  12.7 8.6 %all_gather.12 = bf16[1024,256]{0,1:T(8,128)(2,1)S(1)} all-gather(bf16[256,256]{0,1:T(8,128)(2,1)S(1)} %bitcast.43), channel_id=1, replica_groups=mesh['groups'=2,'tp'=4,'seq'=2,'rep'=2] {'seq','rep'}, dimensions={0}, use_global_device_ids=true | all-gather | bytes 655360 | tf_op jit(solution)/shard_map/all_gather | solution.py:52
  21.3 7.3 %all_gather.13 = bf16[1024,256]{0,1:T(8,128)(2,1)S(1)} all-gather(bf16[256,256]{0,1:T(8,128)(2,1)S(1)} %bitcast.44), channel_id=1, replica_groups=mesh['groups'=2,'tp'=4,'seq'=2,'rep'=2] {'seq','rep'}, dimensions={0}, use_global_device_ids=true | all-gather | bytes 655360 | tf_op jit(solution)/shard_map/all_gather | solution.py:53
  28.6 0.2 broadcast_compare_fusion
  28.8 3.0 fusion
  31.8 4.0 fusion.1
  35.8 4.5 %fusion.9 = bf16[256,2,8,128]{0,3,2,1:T(8,128)(2,1)S(1)} fusion(bf16[1024,2,128,1]{0,2,3,1:T(8,128)(2,1)S(1)} %bitcast.42, f32[2,1024,256,8]{2,1,3,0:T(8,128)S(1)} %get-tuple-element.5, f32[2,8,256]{2,1,0:T(8,128)S(1)} %broadcast_maximum_fusion, pred[256,1024]{0,1:T(8,128)(4,1)S(1)} %broadcast_compare_fusion, f32[256,2,8]{0,2,1:T(8,128)S(1)} %bitcast.45), kind=kOutput, calls=%fused_computation.14 | convolution fusion | flops 1095761920 | bytes 18644992 | tf_op jit(solution)/shard_map/grqk,kgd->grqd/dot_general | solution.py:68
  40.2 173.6 %all-gather.3.cloned.1.call-done = bf16[2048,8192]{1,0:T(8,128)(2,1)} async-done(((bf16[2048,2048]{1,0:T(8,128)(2,1)}), bf16[2048,8192]{1,0:T(8,128)(2,1)}) %all-gather.3.cloned.1.call-update) | async-done | bytes 33554448 | tf_op jit(solution)/shard_map/all_gather | solution.py:82
  213.8 0.0 copy-start.1
  213.8 16.6 %convolution_convert_fusion = bf16[256,8192]{1,0:T(8,128)(2,1)} fusion(bf16[256,2048]{0,1:T(8,128)(2,1)S(1)} %bitcast.40, bf16[2048,8192]{1,0:T(8,128)(2,1)} %all-gather.3.cloned.1.call-done), kind=kOutput, calls=%fused_computation.5 | convolution fusion | flops 8592031744 | bytes 38797312 | tf_op jit(solution)/shard_map/dot_general | solution.py:80
  230.4 0.0 reduce-scatter.2.cloned.1.call-update
  230.4 0.0 all-gather.5.cloned.1.call-start
  230.5 0.7 dynamic-slice_convert_fusion
  231.2 76.2 %reduce-scatter.2.cloned.1.call-done = bf16[256,2048]{1,0:T(8,128)(2,1)} async-done(((bf16[256,8192]{1,0:T(8,128)(2,1)}), bf16[256,2048]{1,0:T(8,128)(2,1)}) %reduce-scatter.2.cloned.1.call-update) | async-done | bytes 1048592 | tf_op jit(solution)/shard_map/reduce_scatter | solution.py:86
  307.3 0.0 copy-done.1
  307.3 1.7 fusion.6
  309.1 0.0 copy-start
  309.1 10.9 %psum.7 = f32[256]{0:T(256)S(1)} all-reduce(f32[256]{0:T(256)S(1)} %get-tuple-element.2), channel_id=1, replica_groups=mesh['groups'=2,'tp'=4,'seq'=2,'rep'=2] {'tp'}, use_global_device_ids=true, to_apply=%region_6.7 | all-reduce | flops 256 | bytes 2048 | tf_op jit(solution)/shard_map/psum | solution.py:91
  320.0 1.3 fusion.8
  321.3 0.0 all-gather.5.cloned.1.call-update
  321.3 79.3 %all-gather.5.cloned.1.call-done = bf16[256,8192]{1,0:T(8,128)(2,1)} async-done(((bf16[256,2048]{1,0:T(8,128)(2,1)}), bf16[256,8192]{1,0:T(8,128)(2,1)}) %all-gather.5.cloned.1.call-update) | async-done | bytes 4194320 | tf_op jit(solution)/shard_map/all_gather | solution.py:94
  400.6 4.6 %copy.34 = bf16[256,8192]{1,0:T(8,128)(2,1)} copy(bf16[256,8192]{1,0:T(8,128)(2,1)} %all-gather.5.cloned.1.call-done) | data formatting | bytes 8388608
  405.3 0.0 copy-done
  (6 shorter events, 0.0 us)
Async XLA Ops:
  7.2 206.7 %all-gather.3.cloned.1.call-start = ((), (), s32[]{:S(2)}) async-start(), calls=%async_computation.1 | async-start | bytes 41943040 | tf_op jit(solution)/shard_map/all_gather | solution.py:82
  7.9 299.4 %reduce-scatter.2.cloned.1.call-start = ((), (), s32[]{:S(2)}) async-start(), calls=%async_computation.2 | async-start | bytes 5242880 | tf_op jit(solution)/shard_map/reduce_scatter | solution.py:86
  213.8 93.5 %copy-start.1 = (bf16[256,2048]{1,0:T(8,128)(2,1)S(1)}, bf16[256,2048]{1,0:T(8,128)(2,1)}, u32[]{:S(2)}) copy-start(bf16[256,2048]{1,0:T(8,128)(2,1)} %param.12) | copy-start | bytes 3145732
  230.4 170.2 %all-gather.5.cloned.1.call-start = ((), (), s32[]{:S(2)}) async-start(), calls=%async_computation.3 | async-start | bytes 5242880 | tf_op jit(solution)/shard_map/all_gather | solution.py:94
  309.1 96.2 %copy-start = (bf16[256,2048]{1,0:T(8,128)(2,1)}, bf16[256,2048]{1,0:T(8,128)(2,1)S(1)}, u32[]{:S(2)}) copy-start(bf16[256,2048]{1,0:T(8,128)(2,1)S(1)} %get-tuple-element.10) | copy-start | bytes 3145732
Sparse Core Ops, SparseCore 0:
  9.6 204.2 all-gather.2
  230.5 76.7 reduce-scatter.1
  321.5 79.1 all-gather.4
where the time goes:
time: 412 us
  waiting for transfers between devices  330 us (80%)
  blocking collectives  26.8 us (7%)
  matrix products  24 us (6%)
  between operations  13.9 us (3%)
  other arithmetic  9.44 us (2%)
  local copies, waits for them, and re-layouts  7.79 us (2%)
    all_gather x1, waiting for transfers between devices, on_device(): lax.all_gather(out_weight, ('seq', 'rep'), axis=1, tiled=True)  174 us
    all_gather x1, waiting for transfers between devices, on_device(): normed = lax.all_gather(normed_part, 'tp', axis=1, tiled=True)  79.3 us
    reduce_scatter x1, waiting for transfers between devices, on_device(): lax.psum_scatter(term.astype(jnp.bfloat16), 'tp', scatter_dimension=1, ti...  76.2 us
    dot_general x1, matrix products, on_device(): jnp.dot(attention, lax.all_gather(out_weight, ('seq', 'rep'), axis=1, til...  16.6 us
    psum x1, blocking collectives, on_device(): square_total = lax.psum(jnp.sum(stream_wide * stream_wide, axis=1), 'tp')  10.9 us
    all_gather x1, blocking collectives, on_device(): key_block = lax.all_gather(key_sel, ('seq', 'rep'), axis=0, tiled=True)  8.62 us
  transfers between devices with their start and end apart: 3, of which 3 were waited for; matrix products, arithmetic and copies ran while one was open for 4% of the time, Pallas kernels for 0%

commit v1 on v0

--- a/solution.py
+++ b/solution.py
@@ -77,21 +77,28 @@
         .reshape(tok_rows, heads_here * head_size)
         .astype(jnp.bfloat16)
     )
-    term = jnp.dot(
-        attention,
-        lax.all_gather(out_weight, ("seq", "rep"), axis=1, tiled=True),
-        preferred_element_type=jnp.float32,
+    tp_size = lax.axis_size("tp")
+    ring = lax.axis_size("seq") * lax.axis_size("rep")
+    part_rows = tok_rows // tp_size
+    width = residual.shape[1]
+    res_rows = lax.all_to_all(
+        residual.reshape(tp_size, part_rows, width), "tp", 0, 0, tiled=True
     )
-    width = residual.shape[1]
-    summed = lax.psum_scatter(
-        term.astype(jnp.bfloat16), "tp", scatter_dimension=1, tiled=True
-    ).astype(jnp.float32)
-    stream = (residual.astype(jnp.float32) + summed).astype(jnp.bfloat16)
-    stream_wide = stream.astype(jnp.float32)
-    square_total = lax.psum(jnp.sum(stream_wide * stream_wide, axis=1), "tp")
-    gain_part = lax.dynamic_slice_in_dim(norm_gain, tp_index * width, width)
-    normed_part = normalize(stream, gain_part, square_total)
-    normed = lax.all_gather(normed_part, "tp", axis=1, tiled=True)
+    everyone = lax.all_gather(attention, ("seq", "rep"), axis=0, tiled=True)
+    term = jnp.dot(everyone, out_weight, preferred_element_type=jnp.float32).astype(jnp.bfloat16)
+    columns = out_weight.shape[1]
+    part = lax.psum_scatter(
+        term.reshape(ring, tp_size, part_rows, columns), "tp", scatter_dimension=1, tiled=False
+    )
+    mine = lax.all_to_all(part, ("seq", "rep"), 0, 0, tiled=True)
+    summed = mine.transpose(1, 0, 2).reshape(part_rows, D).astype(jnp.float32)
+    stream_rows = (
+        res_rows.transpose(1, 0, 2).reshape(part_rows, D).astype(jnp.float32) + summed
+    ).astype(jnp.bfloat16)
+    whole = lax.all_gather(stream_rows, "tp", axis=0, tiled=True)
+    wide = whole.astype(jnp.float32)
+    normed = normalize(whole, norm_gain, jnp.sum(wide * wide, axis=1))
+    stream = lax.dynamic_slice_in_dim(whole, tp_index * width, width, 1)
     return (stream, normed)
 
 

time: 412 us -> 393 us (0.954)
  waiting for transfers between devices: 330 us -> 286 us
  other arithmetic: 9.44 us -> 16.8 us
  blocking collectives: 26.8 us -> 33 us
  starting transfers between devices: 0.12 us -> 4.69 us
    unnamed x3 -> x4, waiting for transfers between devices: 0.71 us -> 171 us
    all_gather x2, waiting for transfers between devices: 253 us -> 115 us  [the longest x1 79 us: on_device(): whole = lax.all_gather(stream_rows, 'tp', axis=0, tiled=True)]
    reduce_scatter x1 -> x0, waiting for transfers between devices: 76.2 us -> none  [on_device(): lax.psum_scatter(term.astype(jnp.bfloat16), 'tp', scatter_dimension=1, ti...]
    all_to_all x0 -> x1, blocking collectives: none -> 17 us  [on_device(): mine = lax.all_to_all(part, ('seq', 'rep'), 0, 0, tiled=True)]
    psum x1 -> x0, blocking collectives: 10.9 us -> none  [on_device(): square_total = lax.psum(jnp.sum(stream_wide * stream_wide, axis=1), 'tp')]
    all_to_all x0 -> x1, starting transfers between devices: none -> 4.61 us  [on_device(): lax.all_to_all(residual.reshape(tp_size, part_rows, width), 'tp', 0, 0, t...]
    dot_general x1, matrix products: 2.95 us -> 7.31 us  [on_device(): jnp.einsum('qgrd,kgd->grqk', grouped, keys_three, preferred_element_type=...]
    reduce_sum x1, other arithmetic: 4 us -> 8.23 us  [on_device(): new_totals = jnp.sum(expo, axis=3)]
  transfers between devices with their start and end apart: 3 -> 4, of which waited for: 3 -> 3; matrix products, arithmetic and copies ran while one was open for 4% -> 1% of each run, Pallas kernels for 0% -> 0%
where the time goes in v1:
time: 393 us; the launch traced here: 392 us
  waiting for transfers between devices  286 us (73%)
  blocking collectives  33 us (8%)
  matrix products  26.5 us (7%)
  other arithmetic  16.8 us (4%)
  between operations  13.9 us (4%)
  local copies, waits for them, and re-layouts  11.5 us (3%)
  starting transfers between devices  4.69 us (1%)
    unnamed x4, waiting for transfers between devices  171 us
    all_gather x1, waiting for transfers between devices, on_device(): whole = lax.all_gather(stream_rows, 'tp', axis=0, tiled=True)  79 us
    all_gather x1, waiting for transfers between devices, on_device(): everyone = lax.all_gather(attention, ('seq', 'rep'), axis=0, tiled=True)  36 us
    all_to_all x1, blocking collectives, on_device(): mine = lax.all_to_all(part, ('seq', 'rep'), 0, 0, tiled=True)  17 us
    dot_general x1, matrix products, on_device(): jnp.dot(everyone, out_weight, preferred_element_type=jnp.float32)  14 us
    all_gather x1, blocking collectives, on_device(): key_block = lax.all_gather(key_sel, ('seq', 'rep'), axis=0, tiled=True)  8.62 us
    reduce_sum x1, other arithmetic, on_device(): new_totals = jnp.sum(expo, axis=3)  8.23 us
  transfers between devices with their start and end apart: 4, of which 3 were waited for; matrix products, arithmetic and copies ran while one was open for 1% of the time, Pallas kernels for 0%

profile of v1, /device:TPU:0, one launch (start us, length us, event | category | flops | bytes accessed | tf_op | source)
XLA Modules:
  0.0 392.4 jit_solution(15278158147778207372)
XLA Ops:
  7.2 0.0 all-gather.3.cloned.1.call-start
  7.2 1.5 constant_dynamic-slice_fusion
  8.7 0.1 copy.43
  8.8 8.6 %all_gather.12 = bf16[1024,256]{0,1:T(8,128)(2,1)S(1)} all-gather(bf16[256,256]{0,1:T(8,128)(2,1)S(1)} %bitcast.60), channel_id=1, replica_groups=mesh['groups'=2,'tp'=4,'seq'=2,'rep'=2] {'seq','rep'}, dimensions={0}, use_global_device_ids=true | all-gather | bytes 655360 | tf_op jit(solution)/shard_map/all_gather | solution.py:52
  17.5 0.7 select_reduce_fusion.1
  18.2 0.7 select_reduce_fusion
  19.0 1.4 copy.45
  20.4 0.2 broadcast_compare_fusion
  20.7 7.3 %fusion = (f32[2,8,256]{2,1,0:T(8,128)S(1)}, f32[2,1024,256,8]{2,1,3,0:T(8,128)}) fusion(pred[256,1024]{0,1:T(8,128)(4,1)S(1)} %broadcast_compare_fusion, bf16[1024,2,128,1]{0,2,3,1:T(8,128)(2,1)S(1)} %bitcast.56, bf16[256,2,8,128]{3,2,1,0:T(8,128)(2,1)S(1)} %bitcast.53), kind=kOutput, calls=%fused_computation.2 | convolution fusion | flops 1086320640 | bytes 18628608 | tf_op jit(solution)/shard_map/qgrd,kgd->grqk/dot_general | solution.py:60
  28.0 0.1 copy.42
  28.1 7.3 %all_gather.13 = bf16[1024,256]{0,1:T(8,128)(2,1)S(1)} all-gather(bf16[256,256]{0,1:T(8,128)(2,1)S(1)} %bitcast.61), channel_id=1, replica_groups=mesh['groups'=2,'tp'=4,'seq'=2,'rep'=2] {'seq','rep'}, dimensions={0}, use_global_device_ids=true | all-gather | bytes 655360 | tf_op jit(solution)/shard_map/all_gather | solution.py:53
  35.4 0.0 copy-start
  35.4 8.2 %fusion.1 = f32[2,8,256]{2,1,0:T(8,128)S(1)} fusion(f32[2,1024,256,8]{2,1,3,0:T(8,128)} %get-tuple-element.3, f32[2,8,256]{2,1,0:T(8,128)S(1)} %broadcast_maximum_fusion, pred[256,1024]{0,1:T(8,128)(4,1)S(1)} %broadcast_compare_fusion), kind=kLoop, calls=%fused_computation.3 | loop fusion | flops 20967424 | bytes 17072128 | tf_op jit(solution)/shard_map/reduce_sum | solution.py:67
  43.6 2.4 copy-done
  46.1 5.2 %fusion.9 = bf16[256,2,8,128]{0,3,2,1:T(8,128)(2,1)} fusion(bf16[1024,2,128,1]{0,2,3,1:T(8,128)(2,1)S(1)} %bitcast.59, f32[2,1024,256,8]{2,1,3,0:T(8,128)S(1)} %copy-done, f32[2,8,256]{2,1,0:T(8,128)S(1)} %broadcast_maximum_fusion, pred[256,1024]{0,1:T(8,128)(4,1)S(1)} %broadcast_compare_fusion, f32[256,2,8]{0,2,1:T(8,128)S(1)} %bitcast.62), kind=kOutput, calls=%fused_computation.14 | convolution fusion | flops 1095761920 | bytes 18644992 | tf_op jit(solution)/shard_map/grqk,kgd->grqd/dot_general | solution.py:68
  51.3 0.0 all-gather.3.cloned.1.call-update
  51.3 0.0 copy-start.3
  51.3 0.0 all-reduce.3.cloned.1.call-start
  51.4 36.0 %all-gather.3.cloned.1.call-done = bf16[1024,2048]{0,1:T(8,128)(2,1)} async-done(((bf16[256,2048]{0,1:T(8,128)(2,1)}), bf16[1024,2048]{0,1:T(8,128)(2,1)}) %all-gather.3.cloned.1.call-update) | async-done | bytes 4194320 | tf_op jit(solution)/shard_map/all_gather | solution.py:87
  87.4 14.0 %convolution_convert_fusion = bf16[1024,2048]{1,0:T(8,128)(2,1)} fusion(bf16[1024,2048]{0,1:T(8,128)(2,1)} %all-gather.3.cloned.1.call-done, bf16[2048,2048]{1,0:T(8,128)(2,1)} %param.11), kind=kOutput, calls=%fused_computation.12 | convolution fusion | flops 8592031744 | bytes 16777216 | tf_op jit(solution)/shard_map/dot_general | solution.py:88
  101.4 0.0 copy-start.2
  101.4 0.0 all-reduce.3.cloned.1.call-update
  101.4 4.6 %all-to-all-start = ((bf16[4,64,2048]{2,1,0:T(8,128)(2,1)}), bf16[4,64,2048]{2,1,0:T(8,128)(2,1)S(1)}, u32[]{:S(2)}, u32[]{:S(2)}) async-start(bf16[4,64,2048]{2,1,0:T(8,128)(2,1)} %bitcast), calls=%async_computation | async-start | bytes 2097152 | tf_op jit(solution)/shard_map/all_to_all | solution.py:84
  106.0 0.0 all-gather.5.cloned.1.call-start
  106.0 0.0 copy-done.3
  106.0 0.6 dynamic-slice
  106.6 171.0 %all-reduce.3.cloned.1.call-done = bf16[4,4,64,2048]{3,2,1,0:T(8,128)(2,1)} async-done(((bf16[4,4,64,2048]{3,2,1,0:T(8,128)(2,1)}), bf16[4,4,64,2048]{3,2,1,0:T(8,128)(2,1)}) %all-reduce.3.cloned.1.call-update) | async-done | bytes 4194320
  277.6 2.0 dynamic-slice_bitcast_fusion
  279.6 0.0 all-to-all-done
  279.6 17.0 %all_to_all.10 = bf16[4,64,2048]{2,1,0:T(8,128)(2,1)S(1)} all-to-all(bf16[4,64,2048]{2,1,0:T(8,128)(2,1)S(1)} %dynamic-slice_bitcast_fusion), channel_id=1, replica_groups=mesh['groups'=2,'tp'=4,'seq'=2,'rep'=2] {'seq','rep'}, dimensions={0} | all-to-all | bytes 2097152 | tf_op jit(solution)/shard_map/all_to_all | solution.py:93
  296.7 0.4 fusion.12
  297.0 1.0 copy.44
  298.1 0.0 all-gather.5.cloned.1.call-update
  298.1 0.0 copy-done.2
  298.1 79.0 %all-gather.5.cloned.1.call-done = bf16[256,8192]{1,0:T(8,128)(2,1)} async-done(((bf16[64,8192]{1,0:T(8,128)(2,1)}), bf16[256,8192]{1,0:T(8,128)(2,1)}) %all-gather.5.cloned.1.call-update) | async-done | bytes 4194320 | tf_op jit(solution)/shard_map/all_gather | solution.py:98
  377.1 0.0 copy-start.1
  377.1 3.3 fusion.3
  380.4 2.3 constant_dynamic-slice_fusion.2
  382.7 0.0 copy-done.1
  382.7 3.2 fusion.5
  (7 shorter events, 0.1 us)
Async XLA Ops:
  7.2 80.2 %all-gather.3.cloned.1.call-start = ((), (), s32[]{:S(2)}) async-start(), calls=%async_computation.2 | async-start | bytes 5242880 | tf_op jit(solution)/shard_map/all_gather | solution.py:87
  35.4 10.7 %copy-start = (f32[2,1024,256,8]{2,1,3,0:T(8,128)S(1)}, f32[2,1024,256,8]{2,1,3,0:T(8,128)}, u32[]{:S(2)}) copy-start(f32[2,1024,256,8]{2,1,3,0:T(8,128)} %get-tuple-element.3) | copy-start | bytes 50331652
  51.3 54.7 %copy-start.3 = (u32[32]{0:T(128)S(1)}, u32[32]{0:T(128)}, u32[]{:S(2)}) copy-start(u32[32]{0:T(128)} %constant.101) | copy-start | bytes 388
  51.3 226.3 %all-reduce.3.cloned.1.call-start = ((), (), s32[]{:S(2)}) async-start(), calls=%async_computation.4 | async-start | bytes 8388608
  101.4 196.7 %copy-start.2 = (bf16[8192]{0:T(1024)(128)(2,1)S(1)}, bf16[8192]{0:T(1024)(128)(2,1)}, u32[]{:S(2)}) copy-start(bf16[8192]{0:T(1024)(128)(2,1)} %param.13) | copy-start | bytes 49156
  101.4 178.2 %all-to-all-start = ((bf16[4,64,2048]{2,1,0:T(8,128)(2,1)}), bf16[4,64,2048]{2,1,0:T(8,128)(2,1)S(1)}, u32[]{:S(2)}, u32[]{:S(2)}) async-start(bf16[4,64,2048]{2,1,0:T(8,128)(2,1)} %bitcast), calls=%async_computation | async-start | bytes 2097152 | tf_op jit(solution)/shard_map/all_to_all | solution.py:84
  106.0 271.1 %all-gather.5.cloned.1.call-start = ((), (), s32[]{:S(2)}) async-start(), calls=%async_computation.3 | async-start | bytes 5242880 | tf_op jit(solution)/shard_map/all_gather | solution.py:98
  377.1 5.6 %copy-start.1 = (bf16[256,8192]{1,0:T(8,128)(2,1)S(1)}, bf16[256,8192]{1,0:T(8,128)(2,1)}, u32[]{:S(2)}) copy-start(bf16[256,8192]{1,0:T(8,128)(2,1)} %all-gather.5.cloned.1.call-done) | copy-start | bytes 12582916
Sparse Core Ops, SparseCore 0:
  51.4 35.8 all-gather.2
  101.5 176.0 all-reduce.2
  298.2 78.8 all-gather.4

commit v2 on v0

--- a/solution.py
+++ b/solution.py
@@ -1,8 +1,11 @@
+import functools
 import math
 
 import jax
 import jax.numpy as jnp
 from jax import lax
+from jax.experimental import pallas as pl
+from jax.experimental.pallas import tpu as pltpu
 from jax.sharding import PartitionSpec as P
 
 D = 8192
@@ -12,6 +15,7 @@
 
 NEG_LARGE = -1e30
 EPS_NORM = 1e-05
+MESH = pl.DeviceIdType.MESH
 
 
 def positions(rows, span_order, span_len):
@@ -25,6 +29,282 @@
     stream_wide = stream_rows.astype(jnp.float32)
     inverse = lax.rsqrt(square_total[:, None] / D + EPS_NORM)
     return (stream_wide * inverse * gain_part.astype(jnp.float32)[None, :]).astype(jnp.bfloat16)
+
+
+def project_kernel(
+    nt, nc, nrep, att, weight, res, gain, stream_o, normed_o,
+    term, from_low, from_high, sums_out, sums_in, res_rows, full,
+    term_send, low_recv, high_recv, sums_send, sums_recv,
+    res_send, res_recv, up_send, down_send, full_recv,
+):
+    chunks, _, _, rows, width = term.shape
+    columns = chunks * width
+    t = lax.axis_index("tp")
+    c = lax.axis_index("seq") * nrep + lax.axis_index("rep")
+    last = nt - 1
+
+    def quad(other):
+        return {"seq": other // nrep, "rep": other % nrep}
+
+    barrier = pltpu.get_barrier_semaphore()
+    for step in range(1, nt):
+        pl.semaphore_signal(
+            barrier, inc=1, device_id={"tp": (t + step) % nt}, device_id_type=MESH
+        )
+    for step in range(1, nc):
+        pl.semaphore_signal(
+            barrier, inc=1, device_id=quad((c + step) % nc), device_id_type=MESH
+        )
+    pl.semaphore_wait(barrier, nt + nc - 2)
+
+    def remote(src, dst, send, recv, where):
+        return pltpu.make_async_remote_copy(
+            src_ref=src, dst_ref=dst, send_sem=send, recv_sem=recv,
+            device_id=where, device_id_type=MESH,
+        )
+
+    def res_copy(step):
+        other = (t + step) % nt
+        return remote(
+            res.at[pl.ds(pl.multiple_of(other * rows, rows), rows)],
+            res_rows.at[t], res_send.at[step], res_recv.at[step], {"tp": other},
+        )
+
+    def term_up(k, d):
+        return remote(term.at[k, d], from_low.at[k, d], term_send.at[k, d],
+                      low_recv.at[k, d], {"tp": (t + 1) % nt})
+
+    def term_down(k, d):
+        return remote(term.at[k, d], from_high.at[k, d], term_send.at[k, d],
+                      high_recv.at[k, d], {"tp": (t + last) % nt})
+
+    def sums_copy(k, step):
+        other = (c + step) % nc
+        return remote(sums_out.at[k, other], sums_in.at[k, c], sums_send.at[k, step],
+                      sums_recv.at[k, step], quad(other))
+
+    def full_up(k, u):
+        return remote(full.at[u, k], full.at[u, k], up_send.at[k, u],
+                      full_recv.at[k, u], {"tp": (t + 1) % nt})
+
+    def full_down(k, u):
+        return remote(full.at[u, k], full.at[u, k], down_send.at[k, u],
+                      full_recv.at[k, u], {"tp": (t + last) % nt})
+
+    def multiply(k):
+        part = weight[:, pl.ds(pl.multiple_of(k * width, width), width)]
+        for d in range(nt):
+            left = att[:, d].reshape(nc * rows, att.shape[3])
+            out = jnp.dot(left, part, preferred_element_type=jnp.float32)
+            term[k, d] = out.astype(jnp.bfloat16).reshape(nc, rows, width)
+
+        @pl.when(t == 0)
+        def _():
+            for d in range(last, 0, -1):
+                term_up(k, d).start()
+
+        @pl.when(t == last)
+        def _():
+            for d in range(last):
+                term_down(k, d).start()
+
+    def add(x, y):
+        return x.astype(jnp.float32) + y.astype(jnp.float32)
+
+    def forward_terms(k):
+        for step in range(last):
+            d_up, d_down = last - step, step
+
+            @pl.when((t > 0) & (t < d_up))
+            def _():
+                term_up(k, d_up).wait_recv()
+                term[k, d_up] = add(term[k, d_up], from_low[k, d_up]).astype(jnp.bfloat16)
+                term_up(k, d_up).start()
+
+            @pl.when((t < last) & (t > d_down))
+            def _():
+                term_down(k, d_down).wait_recv()
+                term[k, d_down] = add(term[k, d_down], from_high[k, d_down]).astype(jnp.bfloat16)
+                term_down(k, d_down).start()
+
+    def finish(k):
+        @pl.when(t > 0)
+        def _():
+            term_up(k, t).wait_recv()
+
+        @pl.when(t < last)
+        def _():
+            term_down(k, t).wait_recv()
+
+        @pl.when(t == 0)
+        def _():
+            sums_out[k] = add(term[k, t], from_high[k, t]).astype(jnp.bfloat16)
+
+        @pl.when(t == last)
+        def _():
+            sums_out[k] = add(term[k, t], from_low[k, t]).astype(jnp.bfloat16)
+
+        @pl.when((t > 0) & (t < last))
+        def _():
+            both = add(term[k, t], from_low[k, t]) + from_high[k, t].astype(jnp.float32)
+            sums_out[k] = both.astype(jnp.bfloat16)
+
+        for step in range(1, nc):
+            sums_copy(k, step).start()
+        sums_in[k, c] = sums_out[k, c]
+
+    def spread(k):
+        for step in range(1, nc):
+            sums_copy(k, step).wait_recv()
+        for block in range(nc):
+            held = res_rows[block, :, pl.ds(pl.multiple_of(k * width, width), width)]
+            full[t, k, block] = add(held, sums_in[k, block]).astype(jnp.bfloat16)
+
+        @pl.when(t < last)
+        def _():
+            full_up(k, t).start()
+
+        @pl.when(t > 0)
+        def _():
+            full_down(k, t).start()
+
+    def forward_full(k):
+        for step in range(1, nt):
+            @pl.when(t >= step)
+            def _():
+                u = t - step
+                full_up(k, u).wait_recv()
+
+                @pl.when(t < last)
+                def _():
+                    full_up(k, u).start()
+
+            @pl.when(t + step <= last)
+            def _():
+                u = t + step
+                full_down(k, u).wait_recv()
+
+                @pl.when(t > 0)
+                def _():
+                    full_down(k, u).start()
+
+    for step in range(1, nt):
+        res_copy(step).start()
+    res_rows[t] = res[pl.ds(pl.multiple_of(t * rows, rows), rows)]
+
+    def tick(at, carry):
+        @pl.when(at < chunks)
+        def _():
+            multiply(at)
+            forward_terms(at)
+
+        @pl.when((at >= 1) & (at <= chunks))
+        def _():
+            finish(at - 1)
+
+        @pl.when(at == 1)
+        def _():
+            for step in range(1, nt):
+                res_copy(step).wait_recv()
+
+        @pl.when(at >= 2)
+        def _():
+            forward_full(at - 2)
+
+        @pl.when((at >= 1) & (at <= chunks))
+        def _():
+            spread(at - 1)
+
+        return carry
+
+    lax.fori_loop(0, chunks + 2, tick, 0)
+
+    def scale_rows(u, carry):
+        def squares(k, total):
+            piece = full[u, k].astype(jnp.float32)
+            return total + jnp.sum(piece * piece, axis=0)
+
+        total = lax.fori_loop(0, chunks, squares, jnp.zeros((rows, width), jnp.float32))
+        inverse = lax.rsqrt(jnp.sum(total, axis=1, keepdims=True) / D + EPS_NORM)
+        here = pl.ds(pl.multiple_of(u * rows, rows), rows)
+
+        def scale(k, inner):
+            for block in range(nc):
+                at = pl.ds(pl.multiple_of(block * columns + k * width, width), width)
+                wide = full[u, k, block].astype(jnp.float32)
+                normed_o[here, at] = (wide * inverse * gain[:, at]).astype(jnp.bfloat16)
+            at = pl.ds(pl.multiple_of(k * width, width), width)
+            stream_o[here, at] = full[u, k, t]
+            return inner
+
+        return lax.fori_loop(0, chunks, scale, carry)
+
+    lax.fori_loop(0, nt, scale_rows, 0)
+
+    for step in range(1, nt):
+        res_copy(step).wait_send()
+
+    def drain(k, carry):
+        for d in range(nt):
+            @pl.when(t != d)
+            def _():
+                term_up(k, d).wait_send()
+
+            @pl.when((t < last) & (t >= d))
+            def _():
+                full_up(k, d).wait_send()
+
+            @pl.when((t > 0) & (t <= d))
+            def _():
+                full_down(k, d).wait_send()
+
+        for step in range(1, nc):
+            sums_copy(k, step).wait_send()
+        return carry
+
+    lax.fori_loop(0, chunks, drain, 0)
+
+
+def project(everyone, out_weight, residual, norm_gain, nt, nc, nrep):
+    tok_rows, columns = residual.shape
+    depth = out_weight.shape[0]
+    rows = tok_rows // nt
+    width = min(256, columns // 4)
+    chunks = columns // width
+    bf16 = jnp.bfloat16
+    dma = pltpu.SemaphoreType.DMA
+    vmem = pl.BlockSpec(memory_space=pltpu.VMEM)
+    return pl.pallas_call(
+        functools.partial(project_kernel, nt, nc, nrep),
+        out_shape=(
+            jax.ShapeDtypeStruct((tok_rows, columns), bf16),
+            jax.ShapeDtypeStruct((tok_rows, D), bf16),
+        ),
+        in_specs=[vmem] * 4,
+        out_specs=(vmem, vmem),
+        scratch_shapes=[
+            pltpu.VMEM((chunks, nt, nc, rows, width), bf16),
+            pltpu.VMEM((chunks, nt, nc, rows, width), bf16),
+            pltpu.VMEM((chunks, nt, nc, rows, width), bf16),
+            pltpu.VMEM((chunks, nc, rows, width), bf16),
+            pltpu.VMEM((chunks, nc, rows, width), bf16),
+            pltpu.VMEM((nt, rows, columns), bf16),
+            pltpu.VMEM((nt, chunks, nc, rows, width), bf16),
+            dma((chunks, nt)), dma((chunks, nt)), dma((chunks, nt)),
+            dma((chunks, nc)), dma((chunks, nc)),
+            dma((nt,)), dma((nt,)),
+            dma((chunks, nt)), dma((chunks, nt)), dma((chunks, nt)),
+        ],
+        compiler_params=pltpu.CompilerParams(
+            collective_id=0, has_side_effects=True, vmem_limit_bytes=56 * 2**20
+        ),
+        cost_estimate=pl.CostEstimate(
+            flops=2 * nc * tok_rows * depth * columns, bytes_accessed=20 * 2**20, transcendentals=0
+        ),
+    )(
+        everyone.reshape(nc, nt, rows, depth), out_weight, residual,
+        norm_gain.astype(jnp.float32).reshape(1, D),
+    )
 
 
 def on_device(queries, keys, values, span_order, out_weight, residual, norm_gain):
@@ -77,22 +357,11 @@
         .reshape(tok_rows, heads_here * head_size)
         .astype(jnp.bfloat16)
     )
-    term = jnp.dot(
-        attention,
-        lax.all_gather(out_weight, ("seq", "rep"), axis=1, tiled=True),
-        preferred_element_type=jnp.float32,
-    )
-    width = residual.shape[1]
-    summed = lax.psum_scatter(
-        term.astype(jnp.bfloat16), "tp", scatter_dimension=1, tiled=True
-    ).astype(jnp.float32)
-    stream = (residual.astype(jnp.float32) + summed).astype(jnp.bfloat16)
-    stream_wide = stream.astype(jnp.float32)
-    square_total = lax.psum(jnp.sum(stream_wide * stream_wide, axis=1), "tp")
-    gain_part = lax.dynamic_slice_in_dim(norm_gain, tp_index * width, width)
-    normed_part = normalize(stream, gain_part, square_total)
-    normed = lax.all_gather(normed_part, "tp", axis=1, tiled=True)
-    return (stream, normed)
+    tp_size = lax.axis_size("tp")
+    rep_size = lax.axis_size("rep")
+    ring = lax.axis_size("seq") * rep_size
+    everyone = lax.all_gather(attention, ("seq", "rep"), axis=0, tiled=True)
+    return project(everyone, out_weight, residual, norm_gain, tp_size, ring, rep_size)
 
 
 def solution(mesh):

time: 412 us -> 325 us (0.79)
  waiting for transfers between devices: 330 us -> 34.9 us
  Pallas kernels: 0 us -> 226 us
  matrix products: 24 us -> 11.8 us
  blocking collectives: 26.8 us -> 16 us
    pallas_call x0 -> x1, Pallas kernels: none -> 226 us  [project(): pl.pallas_call(functools.partial(project_kernel, nt, nc, nrep), out_shape...]
    all_gather x2 -> x1, waiting for transfers between devices: 253 us -> 34.9 us  [on_device(): everyone = lax.all_gather(attention, ('seq', 'rep'), axis=0, tiled=True)]
    reduce_scatter x1 -> x0, waiting for transfers between devices: 76.2 us -> none  [on_device(): lax.psum_scatter(term.astype(jnp.bfloat16), 'tp', scatter_dimension=1, ti...]
    dot_general x1 -> x0, matrix products: 16.6 us -> none  [on_device(): jnp.dot(attention, lax.all_gather(out_weight, ('seq', 'rep'), axis=1, til...]
    psum x1 -> x0, blocking collectives: 10.9 us -> none  [on_device(): square_total = lax.psum(jnp.sum(stream_wide * stream_wide, axis=1), 'tp')]
    dot_general x1, matrix products: 2.95 us -> 7.31 us  [on_device(): jnp.einsum('qgrd,kgd->grqk', grouped, keys_three, preferred_element_type=...]
    unnamed x8 -> x9, local copies, waits for them, and re-layouts: 6.32 us -> 8.62 us
  transfers between devices with their start and end apart: 3 -> 1, of which waited for: 3 -> 1; matrix products, arithmetic and copies ran while one was open for 4% -> 0% of each run, Pallas kernels for 0% -> 0%
where the time goes in v2:
time: 325 us
  Pallas kernels  226 us (70%)
  waiting for transfers between devices  34.9 us (11%)
  blocking collectives  16 us (5%)
  between operations  14.2 us (4%)
  matrix products  11.8 us (4%)
  local copies, waits for them, and re-layouts  11.5 us (4%)
  other arithmetic  10.3 us (3%)
    pallas_call x1, Pallas kernels, project(): pl.pallas_call(functools.partial(project_kernel, nt, nc, nrep), out_shape...  226 us
    all_gather x1, waiting for transfers between devices, on_device(): everyone = lax.all_gather(attention, ('seq', 'rep'), axis=0, tiled=True)  34.9 us
    all_gather x1, blocking collectives, on_device(): key_block = lax.all_gather(key_sel, ('seq', 'rep'), axis=0, tiled=True)  8.62 us
    unnamed x9, local copies, waits for them, and re-layouts  8.62 us
    reduce_sum x1, other arithmetic, on_device(): new_totals = jnp.sum(expo, axis=3)  7.98 us
    all_gather x1, blocking collectives, on_device(): value_block = lax.all_gather(value_sel, ('seq', 'rep'), axis=0, tiled=True)  7.43 us
    dot_general x1, matrix products, on_device(): jnp.einsum('qgrd,kgd->grqk', grouped, keys_three, preferred_element_type=...  7.31 us
  transfers between devices with their start and end apart: 1, of which 1 were waited for; matrix products, arithmetic and copies ran while one was open for 0% of the time, Pallas kernels for 0%

profile of v2, /device:TPU:0, one launch (start us, length us, event | category | flops | bytes accessed | tf_op | source)
XLA Modules:
  0.0 324.6 jit_solution(8342330631958514635)
XLA Ops:
  7.2 0.0 all-gather.2.cloned.1.call-start
  7.2 1.5 constant_dynamic-slice_fusion
  8.7 0.1 copy.30
  8.8 8.6 %all_gather.9 = bf16[1024,256]{0,1:T(8,128)(2,1)S(1)} all-gather(bf16[256,256]{0,1:T(8,128)(2,1)S(1)} %bitcast.43), channel_id=1, replica_groups=mesh['groups'=2,'tp'=4,'seq'=2,'rep'=2] {'seq','rep'}, dimensions={0}, use_global_device_ids=true | all-gather | bytes 655360 | tf_op jit(solution)/shard_map/all_gather | solution.py:332
  17.5 0.7 select_reduce_fusion.1
  18.2 0.7 select_reduce_fusion
  19.0 1.4 copy.31
  20.4 0.2 broadcast_compare_fusion
  20.7 7.3 %fusion = (f32[2,8,256]{2,1,0:T(8,128)S(1)}, f32[2,1024,256,8]{2,1,3,0:T(8,128)}) fusion(pred[256,1024]{0,1:T(8,128)(4,1)S(1)} %broadcast_compare_fusion, bf16[1024,2,128,1]{0,2,3,1:T(8,128)(2,1)S(1)} %bitcast.39, bf16[256,2,8,128]{3,2,1,0:T(8,128)(2,1)S(1)} %bitcast.38), kind=kOutput, calls=%fused_computation.2 | convolution fusion | flops 1086320640 | bytes 18628608 | tf_op jit(solution)/shard_map/qgrd,kgd->grqk/dot_general | solution.py:340
  28.0 0.1 copy.29
  28.1 0.0 copy-start
  28.1 7.4 %all_gather.10 = bf16[1024,256]{0,1:T(8,128)(2,1)S(1)} all-gather(bf16[256,256]{0,1:T(8,128)(2,1)S(1)} %bitcast.44), channel_id=1, replica_groups=mesh['groups'=2,'tp'=4,'seq'=2,'rep'=2] {'seq','rep'}, dimensions={0}, use_global_device_ids=true | all-gather | bytes 655360 | tf_op jit(solution)/shard_map/all_gather | solution.py:333
  35.5 8.0 %fusion.1 = f32[2,8,256]{2,1,0:T(8,128)S(1)} fusion(f32[2,1024,256,8]{2,1,3,0:T(8,128)} %get-tuple-element.3, f32[2,8,256]{2,1,0:T(8,128)S(1)} %broadcast_maximum_fusion, pred[256,1024]{0,1:T(8,128)(4,1)S(1)} %broadcast_compare_fusion), kind=kLoop, calls=%fused_computation.3 | loop fusion | flops 20967424 | bytes 17072128 | tf_op jit(solution)/shard_map/reduce_sum | solution.py:347
  43.5 0.0 copy-done
  43.5 0.0 copy-start.1
  43.5 4.5 %fusion.6 = bf16[256,2,8,128]{0,3,2,1:T(8,128)(2,1)S(1)} fusion(bf16[1024,2,128,1]{0,2,3,1:T(8,128)(2,1)S(1)} %bitcast.42, f32[2,1024,256,8]{2,1,3,0:T(8,128)S(1)} %copy-done, f32[2,8,256]{2,1,0:T(8,128)S(1)} %broadcast_maximum_fusion, pred[256,1024]{0,1:T(8,128)(4,1)S(1)} %broadcast_compare_fusion, f32[256,2,8]{0,2,1:T(8,128)S(1)} %bitcast.46), kind=kOutput, calls=%fused_computation.8 | convolution fusion | flops 1095761920 | bytes 18644992 | tf_op jit(solution)/shard_map/grqk,kgd->grqd/dot_general | solution.py:348
  48.0 1.4 copy.23
  49.4 0.0 all-gather.2.cloned.1.call-update
  49.5 0.0 copy-done.1
  49.5 0.6 reshape.138
  50.1 34.9 %all-gather.2.cloned.1.call-done = bf16[1024,2048]{1,0:T(8,128)(2,1)} async-done(((bf16[256,2048]{1,0:T(8,128)(2,1)}), bf16[1024,2048]{1,0:T(8,128)(2,1)}) %all-gather.2.cloned.1.call-update) | async-done | bytes 4194320 | tf_op jit(solution)/shard_map/all_gather | solution.py:363
  85.0 225.9 %shard_map.86 = (bf16[256,2048]{1,0:T(8,128)(2,1)}, bf16[256,8192]{1,0:T(8,128)(2,1)}) custom-call(bf16[4,4,64,2048]{3,2,1,0:T(8,128)(2,1)} %bitcast.47, bf16[2048,2048]{1,0:T(8,128)(2,1)} %weight.1, bf16[256,2048]{1,0:T(8,128)(2,1)} %res.1, f32[1,8192]{1,0:T(1,128)} %bitcast.45), custom_call_target="tpu_custom_call" | custom-call | flops 8589934592 | bytes 20971520 | tf_op jit(solution)/shard_map/pallas_call | solution.py:277
  310.8 2.3 copy.38
  313.2 4.6 %copy.39 = bf16[256,8192]{1,0:T(8,128)(2,1)} copy(bf16[256,8192]{1,0:T(8,128)(2,1)} %get-tuple-element.9) | data formatting | bytes 8388608
  (5 shorter events, 0.0 us)
Async XLA Ops:
  7.2 77.8 %all-gather.2.cloned.1.call-start = ((), (), s32[]{:S(2)}) async-start(), calls=%async_computation | async-start | bytes 5242880 | tf_op jit(solution)/shard_map/all_gather | solution.py:363
  28.1 15.4 %copy-start = (f32[2,1024,256,8]{2,1,3,0:T(8,128)S(1)}, f32[2,1024,256,8]{2,1,3,0:T(8,128)}, u32[]{:S(2)}) copy-start(f32[2,1024,256,8]{2,1,3,0:T(8,128)} %get-tuple-element.3) | copy-start | bytes 50331652
  43.5 5.9 %copy-start.1 = (bf16[8192]{0:T(1024)(128)(2,1)S(1)}, bf16[8192]{0:T(1024)(128)(2,1)}, u32[]{:S(2)}) copy-start(bf16[8192]{0:T(1024)(128)(2,1)} %param.13) | copy-start | bytes 49156
Sparse Core Ops, SparseCore 0:
  49.6 35.3 all-gather.1

commit v3 on v2

--- a/solution.py
+++ b/solution.py
@@ -15,6 +15,8 @@
 
 NEG_LARGE = -1e30
 EPS_NORM = 1e-05
+LAG_TERMS, LAG_SUMS, LAG_SPREAD, LAG_FULL = 1, 2, 2, 3
+WIDTH = 512
 MESH = pl.DeviceIdType.MESH
 
 
@@ -192,32 +194,26 @@
         res_copy(step).start()
     res_rows[t] = res[pl.ds(pl.multiple_of(t * rows, rows), rows)]
 
-    def tick(at, carry):
-        @pl.when(at < chunks)
-        def _():
-            multiply(at)
-            forward_terms(at)
-
-        @pl.when((at >= 1) & (at <= chunks))
-        def _():
-            finish(at - 1)
-
-        @pl.when(at == 1)
+    def get_res(k):
+        @pl.when(k == 0)
         def _():
             for step in range(1, nt):
                 res_copy(step).wait_recv()
 
-        @pl.when(at >= 2)
-        def _():
-            forward_full(at - 2)
-
-        @pl.when((at >= 1) & (at <= chunks))
-        def _():
-            spread(at - 1)
+    stages = (
+        (0, multiply), (LAG_TERMS, forward_terms), (LAG_SUMS, finish),
+        (LAG_FULL, forward_full), (LAG_SPREAD, get_res), (LAG_SPREAD, spread),
+    )
+
+    def tick(at, carry):
+        for lag, stage in stages:
+            @pl.when((at >= lag) & (at < chunks + lag))
+            def _():
+                stage(at - lag)
 
         return carry
 
-    lax.fori_loop(0, chunks + 2, tick, 0)
+    lax.fori_loop(0, chunks + LAG_FULL, tick, 0)
 
     def scale_rows(u, carry):
         def squares(k, total):
@@ -269,7 +265,7 @@
     tok_rows, columns = residual.shape
     depth = out_weight.shape[0]
     rows = tok_rows // nt
-    width = min(256, columns // 4)
+    width = min(WIDTH, columns // 4)
     chunks = columns // width
     bf16 = jnp.bfloat16
     dma = pltpu.SemaphoreType.DMA
@@ -329,8 +325,10 @@
     )
     grouped = queries.reshape(tok_rows, groups_here, per_group, head_size)
     score_scale = 1.0 / math.sqrt(head_size)
-    key_block = lax.all_gather(key_sel, ("seq", "rep"), axis=0, tiled=True)
-    value_block = lax.all_gather(value_sel, ("seq", "rep"), axis=0, tiled=True)
+    both = lax.all_gather(
+        jnp.concatenate([key_sel, value_sel], axis=1), ("seq", "rep"), axis=0, tiled=True
+    )
+    key_block, value_block = jnp.split(both, 2, axis=1)
     count = key_block.shape[0]
     key_pos = positions(lax.iota(jnp.int32, count), span_order, span_len)
     best = jnp.full((groups_here, per_group, tok_rows), NEG_LARGE, jnp.float32)

time: 325 us -> 276 us (0.85)
  Pallas kernels: 226 us -> 183 us
  blocking collectives: 16 us -> 0 us
  waiting for transfers between devices: 34.9 us -> 50.8 us
  matrix products: 11.8 us -> 7.41 us
    pallas_call x1, Pallas kernels: 226 us -> 183 us  [project(): pl.pallas_call(functools.partial(project_kernel, nt, nc, nrep), out_shape...]
    all_gather x0 -> x1, waiting for transfers between devices: none -> 16.7 us  [on_device(): lax.all_gather(jnp.concatenate([key_sel, value_sel], axis=1), ('seq', 're...]
    all_gather x2 -> x0, blocking collectives: 16 us -> none  [the longest x1 8.62 us: on_device(): key_block = lax.all_gather(key_sel, ('seq', 'rep'), axis=0, tiled=True)]
    dot_general x1, matrix products: 7.31 us -> 2.94 us  [on_device(): jnp.einsum('qgrd,kgd->grqk', grouped, keys_three, preferred_element_type=...]
    reduce_sum x1, other arithmetic: 7.98 us -> 4 us  [on_device(): new_totals = jnp.sum(expo, axis=3)]
    unnamed x9 -> x7, local copies, waits for them, and re-layouts: 8.62 us -> 8.62 us
  transfers between devices with their start and end apart: 1 -> 2, of which waited for: 1 -> 2; matrix products, arithmetic and copies ran while one was open for 0% -> 1% of each run, Pallas kernels for 0% -> 0%
where the time goes in v3:
time: 276 us; the launch traced here: 275 us
  Pallas kernels  183 us (66%)
  waiting for transfers between devices  50.8 us (18%)
  between operations  14.2 us (5%)
  local copies, waits for them, and re-layouts  12.8 us (5%)
  matrix products  7.41 us (3%)
  other arithmetic  7.07 us (3%)
    pallas_call x1, Pallas kernels, project(): pl.pallas_call(functools.partial(project_kernel, nt, nc, nrep), out_shape...  183 us
    all_gather x1, waiting for transfers between devices, on_device(): everyone = lax.all_gather(attention, ('seq', 'rep'), axis=0, tiled=True)  34 us
    all_gather x1, waiting for transfers between devices, on_device(): lax.all_gather(jnp.concatenate([key_sel, value_sel], axis=1), ('seq', 're...  16.7 us
    unnamed x7, local copies, waits for them, and re-layouts  8.62 us
  transfers between devices with their start and end apart: 2, of which 2 were waited for; matrix products, arithmetic and copies ran while one was open for 1% of the time, Pallas kernels for 0%

profile of v3, /device:TPU:0, one launch (start us, length us, event | category | flops | bytes accessed | tf_op | source)
XLA Modules:
  0.0 275.5 jit_solution(12737955914874978553)
XLA Ops:
  7.2 0.0 all-gather.3.cloned.1.call-start
  7.2 1.5 constant_dynamic-slice_fusion
  8.7 0.1 copy.30
  8.8 0.1 copy.29
  8.9 0.7 pad_maximum_fusion
  9.7 0.0 all-gather.3.cloned.1.call-update
  9.7 0.0 all-gather.5.cloned.1.call-start
  9.7 1.5 copy.31
  11.2 0.7 select_reduce_fusion.1
  12.0 0.7 select_reduce_fusion
  12.7 0.2 broadcast_compare_fusion
  13.0 16.7 %all-gather.3.cloned.1.call-done = bf16[1024,512]{0,1:T(8,128)(2,1)} async-done(((bf16[256,512]{0,1:T(8,128)(2,1)}), bf16[1024,512]{0,1:T(8,128)(2,1)}) %all-gather.3.cloned.1.call-update) | async-done | bytes 1048592 | tf_op jit(solution)/shard_map/all_gather | solution.py:328
  29.7 1.3 fusion.24
  31.0 2.9 %fusion = (f32[2,8,256]{2,1,0:T(8,128)S(1)}, f32[2,1024,256,8]{2,1,3,0:T(8,128)S(1)}) fusion(pred[256,1024]{0,1:T(8,128)(4,1)S(1)} %broadcast_compare_fusion, bf16[1024,2,128,1]{0,2,3,1:T(8,128)(2,1)S(1)} %bitcast.39, bf16[256,2,8,128]{3,2,1,0:T(8,128)(2,1)S(1)} %bitcast.38), kind=kOutput, calls=%fused_computation.2 | convolution fusion | flops 1086320640 | bytes 18628608 | tf_op jit(solution)/shard_map/qgrd,kgd->grqk/dot_general | solution.py:338
  33.9 4.0 %fusion.1 = f32[2,8,256]{2,1,0:T(8,128)S(1)} fusion(f32[2,1024,256,8]{2,1,3,0:T(8,128)S(1)} %get-tuple-element.5, f32[2,8,256]{2,1,0:T(8,128)S(1)} %broadcast_maximum_fusion, pred[256,1024]{0,1:T(8,128)(4,1)S(1)} %broadcast_compare_fusion), kind=kLoop, calls=%fused_computation.3 | loop fusion | flops 20967424 | bytes 17072128 | tf_op jit(solution)/shard_map/reduce_sum | solution.py:345
  37.9 0.0 copy-start
  38.0 4.5 %fusion.6 = bf16[256,2,8,128]{0,3,2,1:T(8,128)(2,1)S(1)} fusion(bf16[1024,2,128,1]{0,2,3,1:T(8,128)(2,1)S(1)} %bitcast.44, f32[2,1024,256,8]{2,1,3,0:T(8,128)S(1)} %get-tuple-element.5, f32[2,8,256]{2,1,0:T(8,128)S(1)} %broadcast_maximum_fusion, pred[256,1024]{0,1:T(8,128)(4,1)S(1)} %broadcast_compare_fusion, f32[256,2,8]{0,2,1:T(8,128)S(1)} %bitcast.46), kind=kOutput, calls=%fused_computation.8 | convolution fusion | flops 1095761920 | bytes 18644992 | tf_op jit(solution)/shard_map/grqk,kgd->grqd/dot_general | solution.py:346
  42.4 1.4 copy.23
  43.9 0.0 all-gather.5.cloned.1.call-update
  43.9 0.0 copy-done
  43.9 0.6 reshape.138
  44.5 34.0 %all-gather.5.cloned.1.call-done = bf16[1024,2048]{1,0:T(8,128)(2,1)} async-done(((bf16[256,2048]{1,0:T(8,128)(2,1)}), bf16[1024,2048]{1,0:T(8,128)(2,1)}) %all-gather.5.cloned.1.call-update) | async-done | bytes 4194320 | tf_op jit(solution)/shard_map/all_gather | solution.py:361
  78.5 183.1 %shard_map.86 = (bf16[256,2048]{1,0:T(8,128)(2,1)}, bf16[256,8192]{1,0:T(8,128)(2,1)}) custom-call(bf16[4,4,64,2048]{3,2,1,0:T(8,128)(2,1)} %bitcast.47, bf16[2048,2048]{1,0:T(8,128)(2,1)} %weight.1, bf16[256,2048]{1,0:T(8,128)(2,1)} %res.1, f32[1,8192]{1,0:T(1,128)} %bitcast.45), custom_call_target="tpu_custom_call" | custom-call | flops 8589934592 | bytes 20971520 | tf_op jit(solution)/shard_map/pallas_call | solution.py:273
  261.7 2.3 copy.38
  264.0 4.6 %copy.39 = bf16[256,8192]{1,0:T(8,128)(2,1)} copy(bf16[256,8192]{1,0:T(8,128)(2,1)} %get-tuple-element.11) | data formatting | bytes 8388608
  (5 shorter events, 0.0 us)
Async XLA Ops:
  7.2 22.5 %all-gather.3.cloned.1.call-start = ((), (), s32[]{:S(2)}) async-start(), calls=%async_computation | async-start | bytes 1310720 | tf_op jit(solution)/shard_map/all_gather | solution.py:328
  9.7 68.8 %all-gather.5.cloned.1.call-start = ((), (), s32[]{:S(2)}) async-start(), calls=%async_computation.1 | async-start | bytes 5242880 | tf_op jit(solution)/shard_map/all_gather | solution.py:361
  37.9 5.9 %copy-start = (bf16[8192]{0:T(1024)(128)(2,1)S(1)}, bf16[8192]{0:T(1024)(128)(2,1)}, u32[]{:S(2)}) copy-start(bf16[8192]{0:T(1024)(128)(2,1)} %param.13) | copy-start | bytes 49156
Sparse Core Ops, SparseCore 0:
  10.1 19.5 all-gather.2
  44.0 34.4 all-gather.4

commit v4 on v3

--- a/solution.py
+++ b/solution.py
@@ -34,10 +34,11 @@
 
 
 def project_kernel(
-    nt, nc, nrep, att, weight, res, gain, stream_o, normed_o,
-    term, from_low, from_high, sums_out, sums_in, res_rows, full,
+    nt, nc, nrep, own, weight, res, gain, stream_o, normed_o,
+    att, term, from_low, from_high, sums_out, sums_in, res_rows, full,
     term_send, low_recv, high_recv, sums_send, sums_recv,
     res_send, res_recv, up_send, down_send, full_recv,
+    seq_send, core_send, att_recv,
 ):
     chunks, _, _, rows, width = term.shape
     columns = chunks * width
@@ -93,6 +94,52 @@
         return remote(full.at[u, k], full.at[u, k], down_send.at[k, u],
                       full_recv.at[k, u], {"tp": (t + last) % nt})
 
+    seq, core = lax.axis_index("seq"), lax.axis_index("rep")
+    nseq = nc // nrep
+
+    def across(d, step):
+        return remote(att.at[c, d], att.at[c, d], seq_send.at[d, step],
+                      att_recv.at[d, c], {"seq": (seq + step) % nseq})
+
+    def share(d, place, step):
+        block = place * nrep + core
+        return remote(att.at[block, d], att.at[block, d], core_send.at[d, place, step],
+                      att_recv.at[d, block], {"rep": (core + step) % nrep})
+
+    def arrived(d, block):
+        remote(att.at[block, d], att.at[block, d], seq_send.at[d, 0],
+               att_recv.at[d, block], {"seq": (seq + 1) % nseq}).wait_recv()
+
+    def send_own(d, carry):
+        att[c, d] = own[d]
+        for step in range(1, nseq):
+            across(d, step).start()
+        for step in range(1, nrep):
+            share(d, seq, step).start()
+        return carry
+
+    def pass_on(d, carry):
+        for step in range(1, nseq):
+            place = (seq + nseq - step) % nseq
+            arrived(d, place * nrep + core)
+            for other in range(1, nrep):
+                share(d, place, other).start()
+        return carry
+
+    def collect(d, carry):
+        for other in range(1, nrep):
+            for place in range(nseq):
+                arrived(d, place * nrep + (core + other) % nrep)
+        return carry
+
+    def att_sent(d, carry):
+        for step in range(1, nseq):
+            across(d, step).wait_send()
+        for place in range(nseq):
+            for other in range(1, nrep):
+                share(d, place, other).wait_send()
+        return carry
+
     def multiply(k):
         part = weight[:, pl.ds(pl.multiple_of(k * width, width), width)]
         for d in range(nt):
@@ -190,6 +237,7 @@
                 def _():
                     full_down(k, u).start()
 
+    lax.fori_loop(0, nt, send_own, 0)
     for step in range(1, nt):
         res_copy(step).start()
     res_rows[t] = res[pl.ds(pl.multiple_of(t * rows, rows), rows)]
@@ -204,6 +252,9 @@
         (0, multiply), (LAG_TERMS, forward_terms), (LAG_SUMS, finish),
         (LAG_FULL, forward_full), (LAG_SPREAD, get_res), (LAG_SPREAD, spread),
     )
+
+    lax.fori_loop(0, nt, pass_on, 0)
+    lax.fori_loop(0, nt, collect, 0)
 
     def tick(at, carry):
         for lag, stage in stages:
@@ -259,9 +310,10 @@
         return carry
 
     lax.fori_loop(0, chunks, drain, 0)
-
-
-def project(everyone, out_weight, residual, norm_gain, nt, nc, nrep):
+    lax.fori_loop(0, nt, att_sent, 0)
+
+
+def project(attention, out_weight, residual, norm_gain, nt, nc, nrep):
     tok_rows, columns = residual.shape
     depth = out_weight.shape[0]
     rows = tok_rows // nt
@@ -279,6 +331,7 @@
         in_specs=[vmem] * 4,
         out_specs=(vmem, vmem),
         scratch_shapes=[
+            pltpu.VMEM((nc, nt, rows, depth), bf16),
             pltpu.VMEM((chunks, nt, nc, rows, width), bf16),
             pltpu.VMEM((chunks, nt, nc, rows, width), bf16),
             pltpu.VMEM((chunks, nt, nc, rows, width), bf16),
@@ -290,6 +343,7 @@
             dma((chunks, nc)), dma((chunks, nc)),
             dma((nt,)), dma((nt,)),
             dma((chunks, nt)), dma((chunks, nt)), dma((chunks, nt)),
+            dma((nt, nc // nrep)), dma((nt, nc // nrep, nrep)), dma((nt, nc)),
         ],
         compiler_params=pltpu.CompilerParams(
             collective_id=0, has_side_effects=True, vmem_limit_bytes=56 * 2**20
@@ -298,7 +352,7 @@
             flops=2 * nc * tok_rows * depth * columns, bytes_accessed=20 * 2**20, transcendentals=0
         ),
     )(
-        everyone.reshape(nc, nt, rows, depth), out_weight, residual,
+        attention.reshape(nt, rows, depth), out_weight, residual,
         norm_gain.astype(jnp.float32).reshape(1, D),
     )
 
@@ -358,8 +412,7 @@
     tp_size = lax.axis_size("tp")
     rep_size = lax.axis_size("rep")
     ring = lax.axis_size("seq") * rep_size
-    everyone = lax.all_gather(attention, ("seq", "rep"), axis=0, tiled=True)
-    return project(everyone, out_weight, residual, norm_gain, tp_size, ring, rep_size)
+    return project(attention, out_weight, residual, norm_gain, tp_size, ring, rep_size)
 
 
 def solution(mesh):

time: 276 us -> 256 us (0.928)
  waiting for transfers between devices: 50.8 us -> 15.5 us
  Pallas kernels: 183 us -> 196 us
    all_gather x1 -> x0, waiting for transfers between devices: 34 us -> none  [on_device(): everyone = lax.all_gather(attention, ('seq', 'rep'), axis=0, tiled=True)]
    pallas_call x1, Pallas kernels: 183 us -> 196 us  [project(): pl.pallas_call(functools.partial(project_kernel, nt, nc, nrep), out_shape...]
    unnamed x7 -> x5, local copies, waits for them, and re-layouts: 8.62 us -> 8.61 us
  transfers between devices with their start and end apart: 2 -> 1, of which waited for: 2 -> 1; matrix products, arithmetic and copies ran while one was open for 1% -> 2% of each run, Pallas kernels for 0% -> 0%
where the time goes in v4:
time: 256 us
  Pallas kernels  196 us (77%)
  waiting for transfers between devices  15.5 us (6%)
  between operations  14.2 us (6%)
  local copies, waits for them, and re-layouts  13.3 us (5%)
  matrix products  8.92 us (3%)
  other arithmetic  7.79 us (3%)
    pallas_call x1, Pallas kernels, project(): pl.pallas_call(functools.partial(project_kernel, nt, nc, nrep), out_shape...  196 us
    all_gather x1, waiting for transfers between devices, on_device(): lax.all_gather(jnp.concatenate([key_sel, value_sel], axis=1), ('seq', 're...  15.5 us
    unnamed x5, local copies, waits for them, and re-layouts  8.61 us
    dot_general x1, matrix products, on_device(): jnp.einsum('grqk,kgd->grqd', expo.astype(jnp.bfloat16), values_three, pre...  5.98 us
  transfers between devices with their start and end apart: 1, of which 1 were waited for; matrix products, arithmetic and copies ran while one was open for 2% of the time, Pallas kernels for 0%

profile of v4, /device:TPU:0, one launch (start us, length us, event | category | flops | bytes accessed | tf_op | source)
XLA Modules:
  0.0 255.8 jit_solution(16198775369322617797)
XLA Ops:
  7.2 0.0 all-gather.2.cloned.1.call-start
  7.2 1.5 constant_dynamic-slice_fusion
  8.7 0.1 copy.34
  8.8 0.1 copy.33
  8.9 0.7 pad_maximum_fusion
  9.7 0.0 all-gather.2.cloned.1.call-update
  9.7 1.5 copy.35
  11.2 1.3 reshape.136
  12.5 0.7 select_reduce_fusion.1
  13.3 0.7 select_reduce_fusion
  14.0 0.2 broadcast_compare_fusion
  14.2 15.5 %all-gather.2.cloned.1.call-done = bf16[1024,512]{0,1:T(8,128)(2,1)} async-done(((bf16[256,512]{0,1:T(8,128)(2,1)}), bf16[1024,512]{0,1:T(8,128)(2,1)}) %all-gather.2.cloned.1.call-update) | async-done | bytes 1048592 | tf_op jit(solution)/shard_map/all_gather | solution.py:382
  29.7 1.3 fusion.24
  31.0 2.9 %fusion = (f32[2,8,256]{2,1,0:T(8,128)S(1)}, f32[2,1024,256,8]{2,1,3,0:T(8,128)S(1)}) fusion(pred[256,1024]{0,1:T(8,128)(4,1)S(1)} %broadcast_compare_fusion, bf16[1024,2,128,1]{0,2,3,1:T(8,128)(2,1)S(1)} %bitcast.39, bf16[256,2,8,128]{3,2,1,0:T(8,128)(2,1)S(1)} %bitcast.38), kind=kOutput, calls=%fused_computation.2 | convolution fusion | flops 1086320640 | bytes 18628608 | tf_op jit(solution)/shard_map/qgrd,kgd->grqk/dot_general | solution.py:392
  33.9 4.0 %fusion.1 = f32[2,8,256]{2,1,0:T(8,128)S(1)} fusion(f32[2,1024,256,8]{2,1,3,0:T(8,128)S(1)} %get-tuple-element.5, f32[2,8,256]{2,1,0:T(8,128)S(1)} %broadcast_maximum_fusion, pred[256,1024]{0,1:T(8,128)(4,1)S(1)} %broadcast_compare_fusion), kind=kLoop, calls=%fused_computation.3 | loop fusion | flops 20967424 | bytes 17072128 | tf_op jit(solution)/shard_map/reduce_sum | solution.py:399
  37.9 6.0 %fusion.6 = bf16[256,2,8,128]{3,0,2,1:T(8,128)(2,1)S(1)} fusion(bf16[1024,2,128,1]{0,2,3,1:T(8,128)(2,1)S(1)} %bitcast.43, f32[2,1024,256,8]{2,1,3,0:T(8,128)S(1)} %get-tuple-element.5, f32[2,8,256]{2,1,0:T(8,128)S(1)} %broadcast_maximum_fusion, pred[256,1024]{0,1:T(8,128)(4,1)S(1)} %broadcast_compare_fusion, f32[256,2,8]{0,2,1:T(8,128)S(1)} %bitcast.45), kind=kOutput, calls=%fused_computation.8 | convolution fusion | flops 1095761920 | bytes 18644992 | tf_op jit(solution)/shard_map/grqk,kgd->grqd/dot_general | solution.py:400
  43.9 0.7 copy.25
  44.6 1.3 convert_element_type.13.own
  45.9 196.1 %shard_map.86 = (bf16[256,2048]{1,0:T(8,128)(2,1)}, bf16[256,8192]{1,0:T(8,128)(2,1)}) custom-call(bf16[4,64,2048]{2,1,0:T(8,128)(2,1)} %convert_element_type.13.own, bf16[2048,2048]{1,0:T(8,128)(2,1)} %weight.1, bf16[256,2048]{1,0:T(8,128)(2,1)} %res.1, f32[1,8192]{1,0:T(1,128)} %bitcast.44), custom_call_target="tpu_custom_call" | custom-call | flops 8589934592 | bytes 20971520 | tf_op jit(solution)/shard_map/pallas_call | solution.py:325
  242.0 2.3 copy.42
  244.3 4.6 %copy.43 = bf16[256,8192]{1,0:T(8,128)(2,1)} copy(bf16[256,8192]{1,0:T(8,128)(2,1)} %get-tuple-element.11) | data formatting | bytes 8388608
  (5 shorter events, 0.0 us)
Async XLA Ops:
  7.2 22.5 %all-gather.2.cloned.1.call-start = ((), (), s32[]{:S(2)}) async-start(), calls=%async_computation | async-start | bytes 1310720 | tf_op jit(solution)/shard_map/all_gather | solution.py:382
Sparse Core Ops, SparseCore 0:
  10.1 19.5 all-gather.1
